TPU v7x, 128 devices: a whole 4x4x4 slice. The times are simulated.
128 devices in a mesh: col: 32 (over x, y, core), row: 4 (over z).
Axes of the slice: x: 4, y: 4, z: 4, core: 2. Of those that a mesh axis runs over, the one named last changes fastest.
Arguments:
- rhs: float32 [2, 32, 4, 4096], P(None, None, 'row', 'col'), may hold values from -6 to 6
- u_factor: bfloat16 [64, 160, 2, 256, 128], P('row', 'col'), may hold values from -0.0390625 to 0.0390625
- v_factor: bfloat16 [64, 160, 2, 256, 128], P('row', 'col'), may hold values from -0.375 to 0.375
- ranks: int32 [64, 160], P('row', 'col'), may hold values from 8 to 128, as said below
- assign: int32 [160], replicated, may hold values from 0 to 159, each once
Outputs:
- solution: float32 [2, 32, 40960], P(None, None, 'col')
- residual_estimate: float32 [32], replicated
Inputs may be any that keep to these rules, and one draw needn't show every extreme that they name: `ranks`: every entry is 128 // 16 times a power of two from 1 to 16.
All inputs are finite; a program needn't handle non-finite values.
Results may differ from a plain program's by a relative error of at most 0.0068.
Values may be sent and summed in bfloat16 or wider, within the bound.
A program may use at most 128 MiB of HBM per device.

v0:
```python
import jax
import jax.numpy as jnp
from jax import lax
from jax.sharding import Mesh
from jax.sharding import PartitionSpec as P

ITERS = 2
COL = ("col_0", "col_1", "col_2")
COL_ROW = ("col_0", "col_1", "col_2", "row")


def cut_along(x, dim, devices):
    before, after = (x.shape[:dim], x.shape[dim + 1 :])
    return jnp.moveaxis(x.reshape(*before, devices, -1, *after), dim, 0)


def sent_and_summed(x, axis, dim):
    devices = lax.axis_size(axis)
    tiles = lax.all_to_all(cut_along(x, dim, devices), axis, 0, 0, tiled=True)
    return jnp.sum(tiles.astype(jnp.float32), axis=0)


def in_order(tiles, dim):
    tiles = jnp.moveaxis(tiles, 0, dim)
    dims = tiles.shape
    return tiles.reshape(*dims[:dim], dims[dim] * dims[dim + 1], *dims[dim + 2 :])


def copy_for_each(x, axis):
    copies = jnp.broadcast_to(x, (lax.axis_size(axis), *x.shape))
    return lax.all_to_all(copies, axis, split_axis=0, concat_axis=0, tiled=True)


def collect(x, axis, dim):
    return in_order(copy_for_each(x, axis), dim)


def by_axis(x, axes):
    for axis in axes:
        x = lax.psum(x, axis)
    return x


def over_copies(x, axis):
    everything = copy_for_each(x, axis)
    return jnp.sum(everything.astype(jnp.float32), axis=0)


def over_copies_2(x, axis):
    everything = copy_for_each(x, axis)
    return jnp.sum(everything, axis=0)


def sum_squares(value):
    return jnp.sum(value * value, axis=(0, 2))


def on_device(rhs, u_factor, v_factor, ranks, assign):
    tile_rows = u_factor.shape[0]
    tile_cols = u_factor.shape[1]
    tile_size = u_factor.shape[3]
    rank_cap = u_factor.shape[4]
    sources = rhs.shape[1]
    rank_iota = lax.broadcasted_iota(jnp.int32, (tile_rows, tile_cols, 1, 1, rank_cap), 4)
    mask = (rank_iota < ranks[:, :, None, None, None]).astype(jnp.float32)

    def adjoint_terms(group_data):
        data_b = group_data.reshape(2, sources, tile_rows, tile_size)
        raw = jnp.einsum("ipcnk,dsin->ipcdsk", u_factor, data_b, preferred_element_type=jnp.float32)
        coeff = jnp.stack(
            [raw[:, :, 0, 0] + raw[:, :, 1, 1], raw[:, :, 0, 1] - raw[:, :, 1, 0]], axis=2
        )
        coeff = (coeff * mask).astype(jnp.bfloat16)
        prod = jnp.einsum("ipcnk,ipdsk->cdspn", v_factor, coeff, preferred_element_type=jnp.float32)
        partial_model = jnp.stack([prod[0, 0] + prod[1, 1], prod[0, 1] - prod[1, 0]], axis=0)
        return partial_model.reshape(2, sources, tile_cols * tile_size)

    def adjoint_step(data_hat, v_prev):
        group_data = collect(data_hat.astype(jnp.bfloat16), COL, 2)
        beta_now = jnp.sqrt(by_axis(sum_squares(data_hat), COL_ROW))
        model_sum = over_copies(adjoint_terms(group_data).astype(jnp.bfloat16), "row").astype(
            jnp.float32
        )
        v_hat = model_sum / beta_now[None, :, None] - beta_now[None, :, None] * v_prev
        alpha_now = jnp.sqrt(over_copies_2(sum_squares(v_hat), COL))
        return (
            data_hat / beta_now[None, :, None],
            beta_now,
            v_hat / alpha_now[None, :, None],
            alpha_now,
        )

    data_first = rhs.reshape(2, sources, rhs.shape[3])
    zero_model = jnp.zeros((2, sources, tile_cols * tile_size), jnp.float32)
    u_vec, beta_now, v_vec, alpha_now = adjoint_step(data_first, zero_model)
    w_vec = v_vec
    x_vec = zero_model
    phibar = beta_now
    rhobar = alpha_now
    for iteration in range(ITERS):
        model_b = v_vec.astype(jnp.bfloat16).reshape(2, sources, tile_cols, tile_size)
        forward_raw = jnp.einsum(
            "ipcnk,dspn->ipcdsk", v_factor, model_b, preferred_element_type=jnp.float32
        )
        forward_coeff = jnp.stack(
            [
                forward_raw[:, :, 0, 0] - forward_raw[:, :, 1, 1],
                forward_raw[:, :, 0, 1] + forward_raw[:, :, 1, 0],
            ],
            axis=2,
        )
        forward_coeff = (forward_coeff * mask).astype(jnp.bfloat16)
        forward_prod = jnp.einsum(
            "ipcnk,ipdsk->cdsin", u_factor, forward_coeff, preferred_element_type=jnp.float32
        )
        partial_data = jnp.stack(
            [forward_prod[0, 0] - forward_prod[1, 1], forward_prod[0, 1] + forward_prod[1, 0]],
            axis=0,
        )
        partial_data = partial_data.reshape(2, sources, tile_rows * tile_size)
        data_hat = (
            sent_and_summed(partial_data.astype(jnp.bfloat16), COL, 2)
            - alpha_now[None, :, None] * u_vec
        )
        u_vec, beta_now, v_vec, alpha_now = adjoint_step(data_hat, v_vec)
        rho_now = jnp.sqrt(rhobar * rhobar + beta_now * beta_now)
        cosine = rhobar / rho_now
        sine = beta_now / rho_now
        theta = sine * alpha_now
        rhobar = -cosine * alpha_now
        phi_now = cosine * phibar
        phibar = sine * phibar
        x_vec = x_vec + (phi_now / rho_now)[None, :, None] * w_vec
        w_vec = v_vec - (theta / rho_now)[None, :, None] * w_vec
    all_cols = assign.shape[0]
    natural = lax.axis_index(COL) * tile_cols + jnp.arange(tile_cols, dtype=jnp.int32)
    positions = jnp.arange(all_cols, dtype=jnp.int32)
    where_held = jnp.sum(
        positions[None, :] * (assign[None, :] == natural[:, None]).astype(jnp.int32), axis=1
    )
    share = sources // lax.axis_size("row")
    own_share = lax.dynamic_slice_in_dim(x_vec, lax.axis_index("row") * share, share, 1)
    gathered = collect(own_share, COL, 2)
    gathered = gathered.reshape(2, share, all_cols, tile_size)
    picked = jnp.concatenate(
        [lax.dynamic_slice_in_dim(gathered, where_held[j], 1, axis=2) for j in range(tile_cols)],
        axis=2,
    ).reshape(2, share, tile_cols * tile_size)
    solution = collect(picked, "row", 1)
    return (solution, phibar)


def solution(mesh):
    split = Mesh(
        mesh.devices.reshape(4, 4, 2, mesh.shape["row"]), ("col_0", "col_1", "col_2", "row")
    )
    placed = (
        P(None, None, "row", COL),
        P("row", COL, None, None, None),
        P("row", COL, None, None, None),
        P("row", COL),
        P(),
    )
    return jax.shard_map(
        on_device, mesh=split, in_specs=placed, out_specs=(P(None, None, COL), P()), check_vma=False
    )
```

profile of v0, /device:TPU:0, one launch (start us, length us, event | category | flops | bytes accessed | tf_op | source)
XLA Modules:
  0.0 296.3 jit_solution(509928026007286434)
XLA Ops:
  0.6 0.8 convert_element_type.53
  1.4 0.9 broadcast_in_dim.18
  2.3 7.4 %all-to-all-start = ((bf16[32,2,32,128]{3,2,1,0:T(8,128)(2,1)}), bf16[32,2,32,128]{3,2,1,0:T(8,128)(2,1)S(1)}, u32[]{:S(2)}, u32[]{:S(2)}) async-start(bf16[32,2,32,128]{3,2,1,0:T(8,128)(2,1)} %broadcast_in_dim.18), calls=%async_computation | async-start | bytes 1048576 | tf_op jit(solution)/shard_map/all_to_all | solution.py:31
  9.7 0.8 copy.220
  10.6 10.3 %all-to-all-done = bf16[32,2,32,128]{3,2,1,0:T(8,128)(2,1)S(1)} async-done(((bf16[32,2,32,128]{3,2,1,0:T(8,128)(2,1)}), bf16[32,2,32,128]{3,2,1,0:T(8,128)(2,1)S(1)}, u32[]{:S(2)}, u32[]{:S(2)}) %all-to-all-start) | async-done | bytes 524320 | tf_op jit(solution)/shard_map/all_to_all | solution.py:31
  21.5 6.0 %fusion.29 = f32[16,5,2,2,32,128]{5,4,2,1,3,0:T(8,128)S(1)} fusion(bf16[16,5,2,256,128]{4,3,2,1,0:T(8,128)(2,1)} %param.6, bf16[2,32,16,256,1,1]{3,2,1,0,5,4:T(8,128)(2,1)S(1)} %bitcast.188), kind=kOutput, calls=%fused_computation.27 | convolution fusion | flops 671088640 | bytes 16252928 | tf_op jit(solution)/shard_map/ipcnk,dsin->ipcdsk/dot_general | solution.py:69
  28.3 3.3 %fusion.55 = f32[2,2,32,5,256]{4,2,0,1,3:T(8,128)S(1)} fusion(bf16[16,5,2,256,128]{4,3,2,1,0:T(8,128)(2,1)S(1)} %bitcast.180, f32[16,5,1,32,128]{4,3,1,0,2:T(8,128)S(1)} %fusion.48, f32[16,5,1,32,128]{4,3,1,0,2:T(8,128)S(1)} %fusion.50, f32[16,5,128]{2,1,0:T(8,128)S(1)} %fusion.88), kind=kOutput, calls=%fused_computation.58 | convolution fusion | flops 673054720 | bytes 13803520 | tf_op jit(solution)/shard_map/ipcnk,ipdsk->cdspn/dot_general | solution.py:74
  32.0 0.9 broadcast_in_dim.19
  32.9 5.3 %all-to-all-start.1 = ((bf16[4,2,32,1280]{3,2,1,0:T(8,128)(2,1)}), bf16[4,2,32,1280]{3,2,1,0:T(8,128)(2,1)S(1)}, u32[]{:S(2)}, u32[]{:S(2)}) async-start(bf16[4,2,32,1280]{3,2,1,0:T(8,128)(2,1)} %broadcast_in_dim.19), calls=%async_computation.1 | async-start | bytes 1310720 | tf_op jit(solution)/shard_map/all_to_all | solution.py:31
  38.3 8.9 %psum.84 = f32[32]{0:T(128)S(1)} all-reduce(f32[32]{0:T(128)S(1)} %multiply_reduce_fusion.4), channel_id=1, replica_groups=mesh['col_0'=4,'col_1'=4,'col_2'=2,'row'=4] {'col_0'}, use_global_device_ids=true, to_apply=%region_2.0 | all-reduce | flops 32 | bytes 256 | tf_op jit(solution)/shard_map/psum | solution.py:40
  47.2 9.2 %psum.85 = f32[32]{0:T(128)S(1)} all-reduce(f32[32]{0:T(128)S(1)} %psum.84), channel_id=1, replica_groups=mesh['col_0'=4,'col_1'=4,'col_2'=2,'row'=4] {'col_1'}, use_global_device_ids=true, to_apply=%region_3.0 | all-reduce | flops 32 | bytes 256 | tf_op jit(solution)/shard_map/psum | solution.py:40
  56.4 2.4 psum.86
  58.9 10.9 %psum.87 = f32[32]{0:T(128)S(1)} all-reduce(f32[32]{0:T(128)S(1)} %psum.86), channel_id=1, replica_groups=mesh['col_0'=4,'col_1'=4,'col_2'=2,'row'=4] {'row'}, use_global_device_ids=true, to_apply=%region_5.0 | all-reduce | flops 32 | bytes 256 | tf_op jit(solution)/shard_map/psum | solution.py:40
  70.2 10.5 %all_to_all.52 = f32[32,1,32]{2,1,0:T(1,128)S(1)} all-to-all(f32[32,1,32]{2,1,0:T(1,128)S(1)} %broadcast_in_dim.21), channel_id=1, replica_groups=mesh['col_0'=4,'col_1'=4,'col_2'=2,'row'=4] {'col_0','col_1','col_2'}, dimensions={0} | all-to-all | bytes 8192 | tf_op jit(solution)/shard_map/all_to_all | solution.py:31
  80.7 5.3 %fusion.20 = f32[16,5,2,2,32,128]{5,4,1,0,3,2:T(8,128)S(1)} fusion(f32[2,4,5,8,256]{4,3,2,1,0:T(8,128)S(1)} %bitcast.184, f32[32]{0:T(128)S(1)} %sqrt.30, f32[32]{0:T(128)S(1)} %get-tuple-element.39, f32[32]{0:T(128)S(1)} %get-tuple-element.38, bf16[16,5,2,256,128]{4,3,2,1,0:T(8,128)(2,1)} %param.7), kind=kOutput, calls=%fused_computation.24 | convolution fusion | flops 671416320 | bytes 16056704 | tf_op jit(solution)/shard_map/ipcnk,dspn->ipcdsk/dot_general | solution.py:102
  86.0 1.7 fusion.47
  87.7 4.6 %fusion.32 = f32[2,2,32,16,256]{4,2,0,1,3:T(8,128)S(1)} fusion(bf16[16,5,2,256,128]{4,3,2,1,0:T(8,128)(2,1)S(1)} %bitcast.176, f32[16,5,1,32,128]{4,3,1,0,2:T(8,128)} %get-tuple-element.16, f32[16,5,1,32,128]{4,3,1,0,2:T(8,128)S(1)} %get-tuple-element.15, f32[16,5,128]{2,1,0:T(8,128)S(1)} %fusion.88), kind=kOutput, calls=%fused_computation.28 | convolution fusion | flops 673054720 | bytes 15245312 | tf_op jit(solution)/shard_map/ipcnk,ipdsk->cdsin/dot_general | solution.py:113
  93.3 14.5 %all_to_all.53 = bf16[32,2,32,128]{3,2,1,0:T(8,128)(2,1)S(1)} all-to-all(bf16[32,2,32,128]{3,2,1,0:T(8,128)(2,1)S(1)} %copy.234), channel_id=1, replica_groups=mesh['col_0'=4,'col_1'=4,'col_2'=2,'row'=4] {'col_0','col_1','col_2'}, dimensions={0} | all-to-all | bytes 1048576 | tf_op jit(solution)/shard_map/all_to_all | solution.py:19
  108.2 15.0 %all_to_all.54 = bf16[32,2,32,128]{3,2,1,0:T(8,128)(2,1)S(1)} all-to-all(bf16[32,2,32,128]{3,2,1,0:T(8,128)(2,1)S(1)} %broadcast_in_dim.22), channel_id=1, replica_groups=mesh['col_0'=4,'col_1'=4,'col_2'=2,'row'=4] {'col_0','col_1','col_2'}, dimensions={0} | all-to-all | bytes 1048576 | tf_op jit(solution)/shard_map/all_to_all | solution.py:31
  123.8 5.3 %fusion.26 = f32[16,5,2,2,32,128]{5,4,1,0,3,2:T(8,128)S(1)} fusion(bf16[2,32,16,256,1,1]{3,2,1,0,5,4:T(8,128)(2,1)S(1)} %bitcast.186, bf16[16,5,2,256,128]{4,3,2,1,0:T(8,128)(2,1)} %param.6), kind=kOutput, calls=%fused_computation.26 | convolution fusion | flops 671088640 | bytes 16252928 | tf_op jit(solution)/shard_map/ipcnk,dsin->ipcdsk/dot_general | solution.py:69
  129.8 0.7 slice-done.11
  130.5 3.3 %fusion.60 = f32[2,2,32,5,256]{4,2,0,1,3:T(8,128)S(1)} fusion(bf16[16,5,2,256,128]{4,3,2,1,0:T(8,128)(2,1)S(1)} %bitcast.182, f32[16,5,1,32,128]{4,3,1,0,2:T(8,128)S(1)} %get-tuple-element.14, f32[16,5,1,32,128]{4,3,1,0,2:T(8,128)S(1)} %get-tuple-element.13, f32[16,5,128]{2,1,0:T(8,128)S(1)} %copy-done.2), kind=kOutput, calls=%fused_computation.59 | convolution fusion | flops 673054720 | bytes 13803520 | tf_op jit(solution)/shard_map/ipcnk,ipdsk->cdspn/dot_general | solution.py:74
  134.1 0.9 broadcast_in_dim.23
  135.0 3.5 %all-to-all-start.5 = ((bf16[4,2,32,1280]{3,2,1,0:T(8,128)(2,1)}), bf16[4,2,32,1280]{3,2,1,0:T(8,128)(2,1)S(1)}, u32[]{:S(2)}, u32[]{:S(2)}) async-start(bf16[4,2,32,1280]{3,2,1,0:T(8,128)(2,1)} %broadcast_in_dim.23), calls=%async_computation.5 | async-start | bytes 1310720 | tf_op jit(solution)/shard_map/all_to_all | solution.py:31
  138.5 8.9 %psum.88 = f32[32]{0:T(128)S(1)} all-reduce(f32[32]{0:T(128)S(1)} %get-tuple-element.9), channel_id=1, replica_groups=mesh['col_0'=4,'col_1'=4,'col_2'=2,'row'=4] {'col_0'}, use_global_device_ids=true, to_apply=%region_10.0 | all-reduce | flops 32 | bytes 256 | tf_op jit(solution)/shard_map/psum | solution.py:40
  147.4 9.2 %psum.89 = f32[32]{0:T(128)S(1)} all-reduce(f32[32]{0:T(128)S(1)} %psum.88), channel_id=1, replica_groups=mesh['col_0'=4,'col_1'=4,'col_2'=2,'row'=4] {'col_1'}, use_global_device_ids=true, to_apply=%region_11.0 | all-reduce | flops 32 | bytes 256 | tf_op jit(solution)/shard_map/psum | solution.py:40
  156.6 2.4 psum.90
  159.1 10.9 %psum.91 = f32[32]{0:T(128)S(1)} all-reduce(f32[32]{0:T(128)S(1)} %psum.90), channel_id=1, replica_groups=mesh['col_0'=4,'col_1'=4,'col_2'=2,'row'=4] {'row'}, use_global_device_ids=true, to_apply=%region_13.0 | all-reduce | flops 32 | bytes 256 | tf_op jit(solution)/shard_map/psum | solution.py:40
  170.1 1.1 multiply_reduce_fusion
  171.2 10.3 %all_to_all.55 = f32[32,1,32]{2,1,0:T(1,128)S(1)} all-to-all(f32[32,1,32]{2,1,0:T(1,128)S(1)} %broadcast_in_dim.24), channel_id=1, replica_groups=mesh['col_0'=4,'col_1'=4,'col_2'=2,'row'=4] {'col_0','col_1','col_2'}, dimensions={0} | all-to-all | bytes 8192 | tf_op jit(solution)/shard_map/all_to_all | solution.py:31
  181.6 5.3 %fusion.23 = f32[16,5,2,2,32,128]{5,4,1,0,3,2:T(8,128)S(1)} fusion(f32[2,4,5,8,256]{4,3,2,1,0:T(8,128)S(1)} %bitcast.187, f32[32]{0:T(128)S(1)} %sqrt.33, f32[32]{0:T(128)S(1)} %sqrt.31, f32[2,4,5,8,256]{4,3,2,1,0:T(8,128)S(1)} %bitcast.185, f32[32]{0:T(128)S(1)} %sqrt.30, f32[32]{0:T(128)S(1)} %get-tuple-element.39, f32[32]{0:T(128)S(1)} %get-tuple-element.38, ...), kind=kOutput, calls=%fused_computation.25 | convolution fusion | flops 671744000 | bytes 16384640 | tf_op jit(solution)/shard_map/ipcnk,dspn->ipcdsk/dot_general | solution.py:102
  188.1 3.5 %fusion.35 = f32[2,2,32,16,256]{4,2,0,1,3:T(8,128)S(1)} fusion(bf16[16,5,2,256,128]{4,3,2,1,0:T(8,128)(2,1)S(1)} %bitcast.178, f32[16,5,1,32,128]{4,3,1,0,2:T(8,128)S(1)} %get-tuple-element.12, f32[16,5,1,32,128]{4,3,1,0,2:T(8,128)S(1)} %get-tuple-element.11, f32[16,5,128]{2,1,0:T(8,128)S(1)} %copy-done.2), kind=kOutput, calls=%fused_computation.29 | convolution fusion | flops 673054720 | bytes 15245312 | tf_op jit(solution)/shard_map/ipcnk,ipdsk->cdsin/dot_general | solution.py:113
  192.3 1.0 copy.251
  193.3 3.9 %all-to-all-start.7 = ((bf16[32,2,32,128]{3,2,1,0:T(8,128)(2,1)}), bf16[32,2,32,128]{3,2,1,0:T(8,128)(2,1)S(1)}, u32[]{:S(2)}, u32[]{:S(2)}) async-start(bf16[32,2,32,128]{3,2,1,0:T(8,128)(2,1)} %copy.251), calls=%async_computation.7 | async-start | bytes 1048576 | tf_op jit(solution)/shard_map/all_to_all | solution.py:19
  197.3 11.1 %all-to-all-done.7 = bf16[32,2,32,128]{3,2,1,0:T(8,128)(2,1)S(1)} async-done(((bf16[32,2,32,128]{3,2,1,0:T(8,128)(2,1)}), bf16[32,2,32,128]{3,2,1,0:T(8,128)(2,1)S(1)}, u32[]{:S(2)}, u32[]{:S(2)}) %all-to-all-start.7) | async-done | bytes 524320 | tf_op jit(solution)/shard_map/all_to_all | solution.py:19
  208.6 8.9 %psum.92 = f32[32]{0:T(128)S(1)} all-reduce(f32[32]{0:T(128)S(1)} %multiply_reduce_fusion.2), channel_id=1, replica_groups=mesh['col_0'=4,'col_1'=4,'col_2'=2,'row'=4] {'col_0'}, use_global_device_ids=true, to_apply=%region_19.0 | all-reduce | flops 32 | bytes 256 | tf_op jit(solution)/shard_map/psum | solution.py:40
  217.6 9.2 %psum.93 = f32[32]{0:T(128)S(1)} all-reduce(f32[32]{0:T(128)S(1)} %psum.92), channel_id=1, replica_groups=mesh['col_0'=4,'col_1'=4,'col_2'=2,'row'=4] {'col_1'}, use_global_device_ids=true, to_apply=%region_20.0 | all-reduce | flops 32 | bytes 256 | tf_op jit(solution)/shard_map/psum | solution.py:40
  226.7 2.4 psum.94
  229.2 7.7 %psum.95 = f32[32]{0:T(128)S(1)} all-reduce(f32[32]{0:T(128)S(1)} %psum.94), channel_id=1, replica_groups=mesh['col_0'=4,'col_1'=4,'col_2'=2,'row'=4] {'row'}, use_global_device_ids=true, to_apply=%region_22.0 | all-reduce | flops 32 | bytes 256 | tf_op jit(solution)/shard_map/psum | solution.py:40
  237.7 1.0 fusion.87
  238.7 1.8 broadcast_in_dim.25
  240.5 4.4 %all-to-all-start.8 = ((f32[32,2,8,1280]{3,2,1,0:T(8,128)}), f32[32,2,8,1280]{3,2,1,0:T(8,128)S(1)}, u32[]{:S(2)}, u32[]{:S(2)}) async-start(f32[32,2,8,1280]{3,2,1,0:T(8,128)} %broadcast_in_dim.25), calls=%async_computation.8 | async-start | bytes 5242880 | tf_op jit(solution)/shard_map/all_to_all | solution.py:31
  245.2 0.7 fusion.91
  255.2 24.1 %all-to-all-done.8 = f32[32,2,8,1280]{3,2,1,0:T(8,128)S(1)} async-done(((f32[32,2,8,1280]{3,2,1,0:T(8,128)}), f32[32,2,8,1280]{3,2,1,0:T(8,128)S(1)}, u32[]{:S(2)}, u32[]{:S(2)}) %all-to-all-start.8) | async-done | bytes 2621472 | tf_op jit(solution)/shard_map/all_to_all | solution.py:31
  279.4 3.0 %copy.252 = f32[2,8,32,1280]{3,2,1,0:T(8,128)} copy(f32[2,8,32,1280]{3,1,0,2:T(8,128)S(1)} %bitcast.183) | data formatting | bytes 5242880 | tf_op jit(solution)/shard_map/transpose | solution.py:24
  282.4 2.7 reshape_reshape.11
  285.4 10.1 %all_to_all.56 = f32[4,2,8,1280]{3,2,1,0:T(8,128)S(1)} all-to-all(f32[4,2,8,1280]{3,2,1,0:T(8,128)S(1)} %broadcast_in_dim.52), channel_id=1, replica_groups=mesh['col_0'=4,'col_1'=4,'col_2'=2,'row'=4] {'row'}, dimensions={0} | all-to-all | bytes 655360 | tf_op jit(solution)/shard_map/all_to_all | solution.py:31
  295.5 0.7 copy.367
  (101 shorter events, 8.8 us)
Async XLA Ops:
  2.3 18.6 %all-to-all-start = ((bf16[32,2,32,128]{3,2,1,0:T(8,128)(2,1)}), bf16[32,2,32,128]{3,2,1,0:T(8,128)(2,1)S(1)}, u32[]{:S(2)}, u32[]{:S(2)}) async-start(bf16[32,2,32,128]{3,2,1,0:T(8,128)(2,1)} %broadcast_in_dim.18), calls=%async_computation | async-start | bytes 1048576 | tf_op jit(solution)/shard_map/all_to_all | solution.py:31
  10.6 77.2 %copy-start.1 = (f32[16,5,128]{2,1,0:T(8,128)}, f32[16,5,128]{2,1,0:T(8,128)S(1)}, u32[]{:S(2)}) copy-start(f32[16,5,128]{2,1,0:T(8,128)S(1)} %fusion.88) | copy-start | bytes 122884
  21.2 6.8 %slice-start.6 = ((s8[10485760]{0:T(1024)(128)(4,1)}), s8[2097152]{0:T(1024)(128)(4,1)S(1)}, s32[]{:S(2)}) async-start(s8[10485760]{0:T(1024)(128)(4,1)} %bitcast.179), calls=%async_computation.16 | async-start | bytes 4194304
  21.4 6.6 %slice-start.7 = ((s8[10485760]{0:T(1024)(128)(4,1)}), s8[4194304]{0:T(1024)(128)(4,1)S(1)}, s32[]{:S(2)}) async-start(s8[10485760]{0:T(1024)(128)(4,1)} %bitcast.179), calls=%async_computation.17 | async-start | bytes 8388608
  21.5 6.9 %slice-start.8 = ((s8[10485760]{0:T(1024)(128)(4,1)}), s8[4194304]{0:T(1024)(128)(4,1)S(1)}, s32[]{:S(2)}) async-start(s8[10485760]{0:T(1024)(128)(4,1)} %bitcast.179), calls=%async_computation.18 | async-start | bytes 8388608
  31.6 6.6 %copy-start = (f32[2,32,1,128]{3,2,1,0:T(1,128)S(1)}, f32[2,32,1,128]{3,2,1,0:T(1,128)}, u32[]{:S(2)}) copy-start(f32[2,32,1,128]{3,2,1,0:T(1,128)} %param.5) | copy-start | bytes 98308
  32.9 36.9 %all-to-all-start.1 = ((bf16[4,2,32,1280]{3,2,1,0:T(8,128)(2,1)}), bf16[4,2,32,1280]{3,2,1,0:T(8,128)(2,1)S(1)}, u32[]{:S(2)}, u32[]{:S(2)}) async-start(bf16[4,2,32,1280]{3,2,1,0:T(8,128)(2,1)} %broadcast_in_dim.19), calls=%async_computation.1 | async-start | bytes 1310720 | tf_op jit(solution)/shard_map/all_to_all | solution.py:31
  69.8 17.9 %slice-start = ((s8[10485760]{0:T(1024)(128)(4,1)}), s8[2097152]{0:T(1024)(128)(4,1)S(1)}, s32[]{:S(2)}) async-start(s8[10485760]{0:T(1024)(128)(4,1)} %bitcast.175), calls=%async_computation.10 | async-start | bytes 4194304
  80.7 7.1 %slice-start.1 = ((s8[10485760]{0:T(1024)(128)(4,1)}), s8[4194304]{0:T(1024)(128)(4,1)S(1)}, s32[]{:S(2)}) async-start(s8[10485760]{0:T(1024)(128)(4,1)} %bitcast.175), calls=%async_computation.11 | async-start | bytes 8388608
  80.7 7.1 %slice-start.2 = ((s8[10485760]{0:T(1024)(128)(4,1)}), s8[4194304]{0:T(1024)(128)(4,1)S(1)}, s32[]{:S(2)}) async-start(s8[10485760]{0:T(1024)(128)(4,1)} %bitcast.175), calls=%async_computation.12 | async-start | bytes 8388608
  123.2 6.5 %slice-start.9 = ((s8[10485760]{0:T(1024)(128)(4,1)}), s8[2097152]{0:T(1024)(128)(4,1)S(1)}, s32[]{:S(2)}) async-start(s8[10485760]{0:T(1024)(128)(4,1)} %bitcast.181), calls=%async_computation.19 | async-start | bytes 4194304
  123.8 6.0 %slice-start.10 = ((s8[10485760]{0:T(1024)(128)(4,1)}), s8[4194304]{0:T(1024)(128)(4,1)S(1)}, s32[]{:S(2)}) async-start(s8[10485760]{0:T(1024)(128)(4,1)} %bitcast.181), calls=%async_computation.20 | async-start | bytes 8388608
  123.8 6.7 %slice-start.11 = ((s8[10485760]{0:T(1024)(128)(4,1)}), s8[4194304]{0:T(1024)(128)(4,1)S(1)}, s32[]{:S(2)}) async-start(s8[10485760]{0:T(1024)(128)(4,1)} %bitcast.181), calls=%async_computation.21 | async-start | bytes 8388608
  129.1 1.4 copy-start.2
  135.0 34.9 %all-to-all-start.5 = ((bf16[4,2,32,1280]{3,2,1,0:T(8,128)(2,1)}), bf16[4,2,32,1280]{3,2,1,0:T(8,128)(2,1)S(1)}, u32[]{:S(2)}, u32[]{:S(2)}) async-start(bf16[4,2,32,1280]{3,2,1,0:T(8,128)(2,1)} %broadcast_in_dim.23), calls=%async_computation.5 | async-start | bytes 1310720 | tf_op jit(solution)/shard_map/all_to_all | solution.py:31
  170.0 17.6 %slice-start.3 = ((s8[10485760]{0:T(1024)(128)(4,1)}), s8[2097152]{0:T(1024)(128)(4,1)S(1)}, s32[]{:S(2)}) async-start(s8[10485760]{0:T(1024)(128)(4,1)} %bitcast.177), calls=%async_computation.13 | async-start | bytes 4194304
  181.5 6.0 %slice-start.4 = ((s8[10485760]{0:T(1024)(128)(4,1)}), s8[4194304]{0:T(1024)(128)(4,1)S(1)}, s32[]{:S(2)}) async-start(s8[10485760]{0:T(1024)(128)(4,1)} %bitcast.177), calls=%async_computation.14 | async-start | bytes 8388608
  181.6 6.5 %slice-start.5 = ((s8[10485760]{0:T(1024)(128)(4,1)}), s8[4194304]{0:T(1024)(128)(4,1)S(1)}, s32[]{:S(2)}) async-start(s8[10485760]{0:T(1024)(128)(4,1)} %bitcast.177), calls=%async_computation.15 | async-start | bytes 8388608
  193.3 15.1 %all-to-all-start.7 = ((bf16[32,2,32,128]{3,2,1,0:T(8,128)(2,1)}), bf16[32,2,32,128]{3,2,1,0:T(8,128)(2,1)S(1)}, u32[]{:S(2)}, u32[]{:S(2)}) async-start(bf16[32,2,32,128]{3,2,1,0:T(8,128)(2,1)} %copy.251), calls=%async_computation.7 | async-start | bytes 1048576 | tf_op jit(solution)/shard_map/all_to_all | solution.py:19
  240.5 4.4 %copy-start.3 = (s32[160]{0:T(256)S(1)}, s32[160]{0:T(256)}, u32[]{:S(2)}) copy-start(s32[160]{0:T(256)} %param.9) | copy-start | bytes 1924
  240.5 38.8 %all-to-all-start.8 = ((f32[32,2,8,1280]{3,2,1,0:T(8,128)}), f32[32,2,8,1280]{3,2,1,0:T(8,128)S(1)}, u32[]{:S(2)}, u32[]{:S(2)}) async-start(f32[32,2,8,1280]{3,2,1,0:T(8,128)} %broadcast_in_dim.25), calls=%async_computation.8 | async-start | bytes 5242880 | tf_op jit(solution)/shard_map/all_to_all | solution.py:31
where the time goes:
time: 298 us; the launch traced here: 296 us
  blocking collectives  152 us (51%)
  waiting for transfers between devices  45.6 us (15%)
  matrix products  36.5 us (12%)
  starting transfers between devices  24.5 us (8%)
  local copies, waits for them, and re-layouts  18.5 us (6%)
  between operations  10.6 us (4%)
  other arithmetic  8.95 us (3%)
    psum x12, blocking collectives, by_axis(): x = lax.psum(x, axis)  91.2 us
    all_to_all x4, blocking collectives, copy_for_each(): return lax.all_to_all(copies, axis, split_axis=0, concat_axis=0, tiled=True)  46 us
    all_to_all x4, waiting for transfers between devices, copy_for_each(): return lax.all_to_all(copies, axis, split_axis=0, concat_axis=0, tiled=True)  34.5 us
    all_to_all x4, starting transfers between devices, copy_for_each(): return lax.all_to_all(copies, axis, split_axis=0, concat_axis=0, tiled=True)  20.6 us
    all_to_all x1, blocking collectives, sent_and_summed(): tiles = lax.all_to_all(cut_along(x, dim, devices), axis, 0, 0, tiled=True)  14.5 us
    dot_general x2, matrix products, adjoint_terms(): jnp.einsum('ipcnk,dsin->ipcdsk', u_factor, data_b, preferred_element_type...  11.3 us
    all_to_all x1, waiting for transfers between devices, sent_and_summed(): tiles = lax.all_to_all(cut_along(x, dim, devices), axis, 0, 0, tiled=True)  11.1 us
    dot_general x2, matrix products, on_device(): jnp.einsum('ipcnk,dspn->ipcdsk', v_factor, model_b, preferred_element_typ...  10.6 us
  transfers between devices with their start and end apart: 5, of which 3 were waited for; matrix products, arithmetic and copies ran while one was open for 1% of the time, Pallas kernels for 0%

commit v1 on v0

--- a/solution.py
+++ b/solution.py
@@ -37,7 +37,7 @@
 
 def by_axis(x, axes):
     for axis in axes:
-        x = lax.psum(x, axis)
+        x = jnp.sum(lax.all_gather(x, axis), axis=0)
     return x
 
 

time: 298 us -> 307 us (1.030)
  local copies, waits for them, and re-layouts: 18.5 us -> 24.9 us
    psum x12 -> x0, blocking collectives: 91.2 us -> none  [by_axis(): x = lax.psum(x, axis)]
    unnamed x0 -> x12, blocking collectives: none -> 91 us
    unnamed x33 -> x69, local copies, waits for them, and re-layouts: 2.33 us -> 7.7 us
  transfers between devices with their start and end apart: 5 -> 5, of which waited for: 3 -> 3; matrix products, arithmetic and copies ran while one was open for 1% -> 2% of each run, Pallas kernels for 0% -> 0%
where the time goes in v1:
time: 307 us; the launch traced here: 305 us
  blocking collectives  151 us (49%)
  waiting for transfers between devices  45.8 us (15%)
  matrix products  36.5 us (12%)
  local copies, waits for them, and re-layouts  24.9 us (8%)
  starting transfers between devices  24.3 us (8%)
  between operations  13.4 us (4%)
  other arithmetic  9.21 us (3%)
    unnamed x12, blocking collectives  91 us
    all_to_all x4, blocking collectives, copy_for_each(): return lax.all_to_all(copies, axis, split_axis=0, concat_axis=0, tiled=True)  46 us
    all_to_all x4, waiting for transfers between devices, copy_for_each(): return lax.all_to_all(copies, axis, split_axis=0, concat_axis=0, tiled=True)  34.7 us
    all_to_all x4, starting transfers between devices, copy_for_each(): return lax.all_to_all(copies, axis, split_axis=0, concat_axis=0, tiled=True)  20.4 us
    all_to_all x1, blocking collectives, sent_and_summed(): tiles = lax.all_to_all(cut_along(x, dim, devices), axis, 0, 0, tiled=True)  14.5 us
    dot_general x2, matrix products, adjoint_terms(): jnp.einsum('ipcnk,dsin->ipcdsk', u_factor, data_b, preferred_element_type...  11.3 us
    all_to_all x1, waiting for transfers between devices, sent_and_summed(): tiles = lax.all_to_all(cut_along(x, dim, devices), axis, 0, 0, tiled=True)  11.1 us
    dot_general x2, matrix products, on_device(): jnp.einsum('ipcnk,dspn->ipcdsk', v_factor, model_b, preferred_element_typ...  10.6 us
  transfers between devices with their start and end apart: 5, of which 3 were waited for; matrix products, arithmetic and copies ran while one was open for 2% of the time, Pallas kernels for 0%

profile of v1, /device:TPU:0, one launch (start us, length us, event | category | flops | bytes accessed | tf_op | source)
XLA Modules:
  0.0 305.5 jit_solution(12670647225534586219)
XLA Ops:
  0.6 0.8 convert_element_type.53
  1.4 0.9 broadcast_in_dim.18
  2.3 7.4 %all-to-all-start = ((bf16[32,2,32,128]{3,2,1,0:T(8,128)(2,1)}), bf16[32,2,32,128]{3,2,1,0:T(8,128)(2,1)S(1)}, u32[]{:S(2)}, u32[]{:S(2)}) async-start(bf16[32,2,32,128]{3,2,1,0:T(8,128)(2,1)} %broadcast_in_dim.18), calls=%async_computation | async-start | bytes 1048576 | tf_op jit(solution)/shard_map/all_to_all | solution.py:31
  9.7 0.8 copy.220
  10.6 10.3 %all-to-all-done = bf16[32,2,32,128]{3,2,1,0:T(8,128)(2,1)S(1)} async-done(((bf16[32,2,32,128]{3,2,1,0:T(8,128)(2,1)}), bf16[32,2,32,128]{3,2,1,0:T(8,128)(2,1)S(1)}, u32[]{:S(2)}, u32[]{:S(2)}) %all-to-all-start) | async-done | bytes 524320 | tf_op jit(solution)/shard_map/all_to_all | solution.py:31
  21.5 6.0 %fusion.29 = f32[16,5,2,2,32,128]{5,4,2,1,3,0:T(8,128)S(1)} fusion(bf16[16,5,2,256,128]{4,3,2,1,0:T(8,128)(2,1)} %param.6, bf16[2,32,16,256,1,1]{3,2,1,0,5,4:T(8,128)(2,1)S(1)} %bitcast.192), kind=kOutput, calls=%fused_computation.27 | convolution fusion | flops 671088640 | bytes 16252928 | tf_op jit(solution)/shard_map/ipcnk,dsin->ipcdsk/dot_general | solution.py:69
  28.3 3.3 %fusion.55 = f32[2,2,32,5,256]{4,2,0,1,3:T(8,128)S(1)} fusion(bf16[16,5,2,256,128]{4,3,2,1,0:T(8,128)(2,1)S(1)} %bitcast.184, f32[16,5,1,32,128]{4,3,1,0,2:T(8,128)S(1)} %fusion.48, f32[16,5,1,32,128]{4,3,1,0,2:T(8,128)S(1)} %fusion.50, f32[16,5,128]{2,1,0:T(8,128)S(1)} %fusion.88), kind=kOutput, calls=%fused_computation.58 | convolution fusion | flops 673054720 | bytes 13803520 | tf_op jit(solution)/shard_map/ipcnk,ipdsk->cdspn/dot_general | solution.py:74
  32.1 0.9 broadcast_in_dim.19
  32.9 5.3 %all-to-all-start.1 = ((bf16[4,2,32,1280]{3,2,1,0:T(8,128)(2,1)}), bf16[4,2,32,1280]{3,2,1,0:T(8,128)(2,1)S(1)}, u32[]{:S(2)}, u32[]{:S(2)}) async-start(bf16[4,2,32,1280]{3,2,1,0:T(8,128)(2,1)} %broadcast_in_dim.19), calls=%async_computation.1 | async-start | bytes 1310720 | tf_op jit(solution)/shard_map/all_to_all | solution.py:31
  39.9 8.8 %all-reduce = f32[128]{0:T(128)S(1)} all-reduce(f32[128]{0:T(128)S(1)} %dynamic-update-slice), channel_id=2, replica_groups=mesh['col_0'=4,'col_1'=4,'col_2'=2,'row'=4] {'col_0'}, use_global_device_ids=true, to_apply=%add | all-reduce | flops 128 | bytes 1024
  50.3 9.2 %all-reduce.1 = f32[128]{0:T(128)S(1)} all-reduce(f32[128]{0:T(128)S(1)} %dynamic-update-slice.1), channel_id=3, replica_groups=mesh['col_0'=4,'col_1'=4,'col_2'=2,'row'=4] {'col_1'}, use_global_device_ids=true, to_apply=%add.1 | all-reduce | flops 128 | bytes 1024
  61.1 2.4 all-reduce.2
  65.3 10.9 %all-reduce.3 = f32[128]{0:T(128)S(1)} all-reduce(f32[128]{0:T(128)S(1)} %dynamic-update-slice.3), channel_id=5, replica_groups=mesh['col_0'=4,'col_1'=4,'col_2'=2,'row'=4] {'row'}, use_global_device_ids=true, to_apply=%add.3 | all-reduce | flops 128 | bytes 1024
  76.7 10.5 %all_to_all.55 = f32[32,1,32]{2,1,0:T(1,128)S(1)} all-to-all(f32[32,1,32]{2,1,0:T(1,128)S(1)} %broadcast_in_dim.21), channel_id=1, replica_groups=mesh['col_0'=4,'col_1'=4,'col_2'=2,'row'=4] {'col_0','col_1','col_2'}, dimensions={0} | all-to-all | bytes 8192 | tf_op jit(solution)/shard_map/all_to_all | solution.py:31
  87.2 5.3 %fusion.20 = f32[16,5,2,2,32,128]{5,4,1,0,3,2:T(8,128)S(1)} fusion(f32[2,4,5,8,256]{4,3,2,1,0:T(8,128)S(1)} %bitcast.188, f32[32]{0:T(128)S(1)} %sqrt.88, f32[32]{0:T(128)S(1)} %get-tuple-element.39, f32[32]{0:T(128)S(1)} %get-tuple-element.38, bf16[16,5,2,256,128]{4,3,2,1,0:T(8,128)(2,1)} %param.7), kind=kOutput, calls=%fused_computation.24 | convolution fusion | flops 671416320 | bytes 16056704 | tf_op jit(solution)/shard_map/ipcnk,dspn->ipcdsk/dot_general | solution.py:102
  92.5 1.7 fusion.47
  94.2 4.6 %fusion.32 = f32[2,2,32,16,256]{4,2,0,1,3:T(8,128)S(1)} fusion(bf16[16,5,2,256,128]{4,3,2,1,0:T(8,128)(2,1)S(1)} %bitcast.180, f32[16,5,1,32,128]{4,3,1,0,2:T(8,128)} %get-tuple-element.16, f32[16,5,1,32,128]{4,3,1,0,2:T(8,128)S(1)} %get-tuple-element.15, f32[16,5,128]{2,1,0:T(8,128)S(1)} %fusion.88), kind=kOutput, calls=%fused_computation.28 | convolution fusion | flops 673054720 | bytes 15245312 | tf_op jit(solution)/shard_map/ipcnk,ipdsk->cdsin/dot_general | solution.py:113
  99.8 14.5 %all_to_all.52 = bf16[32,2,32,128]{3,2,1,0:T(8,128)(2,1)S(1)} all-to-all(bf16[32,2,32,128]{3,2,1,0:T(8,128)(2,1)S(1)} %copy.234), channel_id=1, replica_groups=mesh['col_0'=4,'col_1'=4,'col_2'=2,'row'=4] {'col_0','col_1','col_2'}, dimensions={0} | all-to-all | bytes 1048576 | tf_op jit(solution)/shard_map/all_to_all | solution.py:19
  114.7 15.0 %all_to_all.53 = bf16[32,2,32,128]{3,2,1,0:T(8,128)(2,1)S(1)} all-to-all(bf16[32,2,32,128]{3,2,1,0:T(8,128)(2,1)S(1)} %broadcast_in_dim.22), channel_id=1, replica_groups=mesh['col_0'=4,'col_1'=4,'col_2'=2,'row'=4] {'col_0','col_1','col_2'}, dimensions={0} | all-to-all | bytes 1048576 | tf_op jit(solution)/shard_map/all_to_all | solution.py:31
  130.3 5.3 %fusion.26 = f32[16,5,2,2,32,128]{5,4,1,0,3,2:T(8,128)S(1)} fusion(bf16[2,32,16,256,1,1]{3,2,1,0,5,4:T(8,128)(2,1)S(1)} %bitcast.190, bf16[16,5,2,256,128]{4,3,2,1,0:T(8,128)(2,1)} %param.6), kind=kOutput, calls=%fused_computation.26 | convolution fusion | flops 671088640 | bytes 16252928 | tf_op jit(solution)/shard_map/ipcnk,dsin->ipcdsk/dot_general | solution.py:69
  136.3 0.7 slice-done.11
  136.9 3.3 %fusion.60 = f32[2,2,32,5,256]{4,2,0,1,3:T(8,128)S(1)} fusion(bf16[16,5,2,256,128]{4,3,2,1,0:T(8,128)(2,1)S(1)} %bitcast.186, f32[16,5,1,32,128]{4,3,1,0,2:T(8,128)S(1)} %get-tuple-element.14, f32[16,5,1,32,128]{4,3,1,0,2:T(8,128)S(1)} %get-tuple-element.13, f32[16,5,128]{2,1,0:T(8,128)S(1)} %copy-done.2), kind=kOutput, calls=%fused_computation.59 | convolution fusion | flops 673054720 | bytes 13803520 | tf_op jit(solution)/shard_map/ipcnk,ipdsk->cdspn/dot_general | solution.py:74
  140.6 0.9 broadcast_in_dim.23
  141.5 3.5 %all-to-all-start.5 = ((bf16[4,2,32,1280]{3,2,1,0:T(8,128)(2,1)}), bf16[4,2,32,1280]{3,2,1,0:T(8,128)(2,1)S(1)}, u32[]{:S(2)}, u32[]{:S(2)}) async-start(bf16[4,2,32,1280]{3,2,1,0:T(8,128)(2,1)} %broadcast_in_dim.23), calls=%async_computation.5 | async-start | bytes 1310720 | tf_op jit(solution)/shard_map/all_to_all | solution.py:31
  145.2 8.8 %all-reduce.4 = f32[128]{0:T(128)S(1)} all-reduce(f32[128]{0:T(128)S(1)} %dynamic-update-slice.4), channel_id=6, replica_groups=mesh['col_0'=4,'col_1'=4,'col_2'=2,'row'=4] {'col_0'}, use_global_device_ids=true, to_apply=%add.4 | all-reduce | flops 128 | bytes 1024
  154.4 9.2 %all-reduce.5 = f32[128]{0:T(128)S(1)} all-reduce(f32[128]{0:T(128)S(1)} %dynamic-update-slice.5), channel_id=7, replica_groups=mesh['col_0'=4,'col_1'=4,'col_2'=2,'row'=4] {'col_1'}, use_global_device_ids=true, to_apply=%add.5 | all-reduce | flops 128 | bytes 1024
  164.0 2.4 all-reduce.6
  166.8 10.8 %all-reduce.7 = f32[128]{0:T(128)S(1)} all-reduce(f32[128]{0:T(128)S(1)} %dynamic-update-slice.7), channel_id=9, replica_groups=mesh['col_0'=4,'col_1'=4,'col_2'=2,'row'=4] {'row'}, use_global_device_ids=true, to_apply=%add.7 | all-reduce | flops 128 | bytes 1024
  177.9 1.1 multiply_reduce_fusion
  179.0 10.3 %all_to_all.56 = f32[32,1,32]{2,1,0:T(1,128)S(1)} all-to-all(f32[32,1,32]{2,1,0:T(1,128)S(1)} %broadcast_in_dim.24), channel_id=1, replica_groups=mesh['col_0'=4,'col_1'=4,'col_2'=2,'row'=4] {'col_0','col_1','col_2'}, dimensions={0} | all-to-all | bytes 8192 | tf_op jit(solution)/shard_map/all_to_all | solution.py:31
  189.4 5.3 %fusion.23 = f32[16,5,2,2,32,128]{5,4,1,0,3,2:T(8,128)S(1)} fusion(f32[2,4,5,8,256]{4,3,2,1,0:T(8,128)S(1)} %bitcast.191, f32[32]{0:T(128)S(1)} %sqrt.91, f32[32]{0:T(128)S(1)} %sqrt.89, f32[2,4,5,8,256]{4,3,2,1,0:T(8,128)S(1)} %bitcast.189, f32[32]{0:T(128)S(1)} %sqrt.88, f32[32]{0:T(128)S(1)} %get-tuple-element.39, f32[32]{0:T(128)S(1)} %get-tuple-element.38, ...), kind=kOutput, calls=%fused_computation.25 | convolution fusion | flops 671744000 | bytes 16384640 | tf_op jit(solution)/shard_map/ipcnk,dspn->ipcdsk/dot_general | solution.py:102
  195.9 3.5 %fusion.35 = f32[2,2,32,16,256]{4,2,0,1,3:T(8,128)S(1)} fusion(bf16[16,5,2,256,128]{4,3,2,1,0:T(8,128)(2,1)S(1)} %bitcast.182, f32[16,5,1,32,128]{4,3,1,0,2:T(8,128)S(1)} %get-tuple-element.12, f32[16,5,1,32,128]{4,3,1,0,2:T(8,128)S(1)} %get-tuple-element.11, f32[16,5,128]{2,1,0:T(8,128)S(1)} %copy-done.2), kind=kOutput, calls=%fused_computation.29 | convolution fusion | flops 673054720 | bytes 15245312 | tf_op jit(solution)/shard_map/ipcnk,ipdsk->cdsin/dot_general | solution.py:113
  200.1 1.0 copy.251
  201.1 3.9 %all-to-all-start.7 = ((bf16[32,2,32,128]{3,2,1,0:T(8,128)(2,1)}), bf16[32,2,32,128]{3,2,1,0:T(8,128)(2,1)S(1)}, u32[]{:S(2)}, u32[]{:S(2)}) async-start(bf16[32,2,32,128]{3,2,1,0:T(8,128)(2,1)} %copy.251), calls=%async_computation.7 | async-start | bytes 1048576 | tf_op jit(solution)/shard_map/all_to_all | solution.py:19
  205.1 11.1 %all-to-all-done.7 = bf16[32,2,32,128]{3,2,1,0:T(8,128)(2,1)S(1)} async-done(((bf16[32,2,32,128]{3,2,1,0:T(8,128)(2,1)}), bf16[32,2,32,128]{3,2,1,0:T(8,128)(2,1)S(1)}, u32[]{:S(2)}, u32[]{:S(2)}) %all-to-all-start.7) | async-done | bytes 524320 | tf_op jit(solution)/shard_map/all_to_all | solution.py:19
  216.7 8.9 %all-reduce.8 = f32[128]{0:T(128)S(1)} all-reduce(f32[128]{0:T(128)S(1)} %dynamic-update-slice.8), channel_id=10, replica_groups=mesh['col_0'=4,'col_1'=4,'col_2'=2,'row'=4] {'col_0'}, use_global_device_ids=true, to_apply=%add.8 | all-reduce | flops 128 | bytes 1024
  226.0 9.2 %all-reduce.9 = f32[128]{0:T(128)S(1)} all-reduce(f32[128]{0:T(128)S(1)} %dynamic-update-slice.9), channel_id=11, replica_groups=mesh['col_0'=4,'col_1'=4,'col_2'=2,'row'=4] {'col_1'}, use_global_device_ids=true, to_apply=%add.9 | all-reduce | flops 128 | bytes 1024
  235.5 2.4 all-reduce.10
  238.3 7.7 %all-reduce.11 = f32[128]{0:T(128)S(1)} all-reduce(f32[128]{0:T(128)S(1)} %dynamic-update-slice.11), channel_id=13, replica_groups=mesh['col_0'=4,'col_1'=4,'col_2'=2,'row'=4] {'row'}, use_global_device_ids=true, to_apply=%add.11 | all-reduce | flops 128 | bytes 1024
  246.9 1.0 fusion.87
  247.9 1.8 broadcast_in_dim.25
  249.7 4.2 %all-to-all-start.8 = ((f32[32,2,8,1280]{3,2,1,0:T(8,128)}), f32[32,2,8,1280]{3,2,1,0:T(8,128)S(1)}, u32[]{:S(2)}, u32[]{:S(2)}) async-start(f32[32,2,8,1280]{3,2,1,0:T(8,128)} %broadcast_in_dim.25), calls=%async_computation.8 | async-start | bytes 5242880 | tf_op jit(solution)/shard_map/all_to_all | solution.py:31
  254.1 0.7 fusion.91
  264.2 24.4 %all-to-all-done.8 = f32[32,2,8,1280]{3,2,1,0:T(8,128)S(1)} async-done(((f32[32,2,8,1280]{3,2,1,0:T(8,128)}), f32[32,2,8,1280]{3,2,1,0:T(8,128)S(1)}, u32[]{:S(2)}, u32[]{:S(2)}) %all-to-all-start.8) | async-done | bytes 2621472 | tf_op jit(solution)/shard_map/all_to_all | solution.py:31
  288.5 3.0 copy.252
  291.6 2.7 reshape_reshape.11
  294.6 10.1 %all_to_all.54 = f32[4,2,8,1280]{3,2,1,0:T(8,128)S(1)} all-to-all(f32[4,2,8,1280]{3,2,1,0:T(8,128)S(1)} %broadcast_in_dim.52), channel_id=1, replica_groups=mesh['col_0'=4,'col_1'=4,'col_2'=2,'row'=4] {'row'}, dimensions={0} | all-to-all | bytes 655360 | tf_op jit(solution)/shard_map/all_to_all | solution.py:31
  304.7 0.7 copy.367
  (161 shorter events, 15.5 us)
Async XLA Ops:
  2.3 18.6 %all-to-all-start = ((bf16[32,2,32,128]{3,2,1,0:T(8,128)(2,1)}), bf16[32,2,32,128]{3,2,1,0:T(8,128)(2,1)S(1)}, u32[]{:S(2)}, u32[]{:S(2)}) async-start(bf16[32,2,32,128]{3,2,1,0:T(8,128)(2,1)} %broadcast_in_dim.18), calls=%async_computation | async-start | bytes 1048576 | tf_op jit(solution)/shard_map/all_to_all | solution.py:31
  10.6 83.6 %copy-start.1 = (f32[16,5,128]{2,1,0:T(8,128)}, f32[16,5,128]{2,1,0:T(8,128)S(1)}, u32[]{:S(2)}) copy-start(f32[16,5,128]{2,1,0:T(8,128)S(1)} %fusion.88) | copy-start | bytes 122884
  21.2 6.8 %slice-start.6 = ((s8[10485760]{0:T(1024)(128)(4,1)}), s8[2097152]{0:T(1024)(128)(4,1)S(1)}, s32[]{:S(2)}) async-start(s8[10485760]{0:T(1024)(128)(4,1)} %bitcast.183), calls=%async_computation.16 | async-start | bytes 4194304
  21.4 6.6 %slice-start.7 = ((s8[10485760]{0:T(1024)(128)(4,1)}), s8[4194304]{0:T(1024)(128)(4,1)S(1)}, s32[]{:S(2)}) async-start(s8[10485760]{0:T(1024)(128)(4,1)} %bitcast.183), calls=%async_computation.17 | async-start | bytes 8388608
  21.5 6.9 %slice-start.8 = ((s8[10485760]{0:T(1024)(128)(4,1)}), s8[4194304]{0:T(1024)(128)(4,1)S(1)}, s32[]{:S(2)}) async-start(s8[10485760]{0:T(1024)(128)(4,1)} %bitcast.183), calls=%async_computation.18 | async-start | bytes 8388608
  31.6 6.7 %copy-start.7 = (u32[128]{0:T(128)S(1)}, u32[128]{0:T(128)}, u32[]{:S(2)}) copy-start(u32[128]{0:T(128)} %constant.38) | copy-start | bytes 1540
  31.6 7.9 %copy-start = (f32[2,32,1,128]{3,2,1,0:T(1,128)S(1)}, f32[2,32,1,128]{3,2,1,0:T(1,128)}, u32[]{:S(2)}) copy-start(f32[2,32,1,128]{3,2,1,0:T(1,128)} %param.5) | copy-start | bytes 98308
  31.6 17.2 %copy-start.6 = (u32[128]{0:T(128)S(1)}, u32[128]{0:T(128)}, u32[]{:S(2)}) copy-start(u32[128]{0:T(128)} %constant.43) | copy-start | bytes 1540
  31.6 28.0 %copy-start.5 = (u32[128]{0:T(128)S(1)}, u32[128]{0:T(128)}, u32[]{:S(2)}) copy-start(u32[128]{0:T(128)} %constant.48) | copy-start | bytes 1540
  31.6 32.0 %copy-start.4 = (u32[128]{0:T(128)S(1)}, u32[128]{0:T(128)}, u32[]{:S(2)}) copy-start(u32[128]{0:T(128)} %constant.53) | copy-start | bytes 1540
  32.9 43.4 %all-to-all-start.1 = ((bf16[4,2,32,1280]{3,2,1,0:T(8,128)(2,1)}), bf16[4,2,32,1280]{3,2,1,0:T(8,128)(2,1)S(1)}, u32[]{:S(2)}, u32[]{:S(2)}) async-start(bf16[4,2,32,1280]{3,2,1,0:T(8,128)(2,1)} %broadcast_in_dim.19), calls=%async_computation.1 | async-start | bytes 1310720 | tf_op jit(solution)/shard_map/all_to_all | solution.py:31
  76.3 17.9 %slice-start = ((s8[10485760]{0:T(1024)(128)(4,1)}), s8[2097152]{0:T(1024)(128)(4,1)S(1)}, s32[]{:S(2)}) async-start(s8[10485760]{0:T(1024)(128)(4,1)} %bitcast.179), calls=%async_computation.10 | async-start | bytes 4194304
  87.2 7.1 %slice-start.1 = ((s8[10485760]{0:T(1024)(128)(4,1)}), s8[4194304]{0:T(1024)(128)(4,1)S(1)}, s32[]{:S(2)}) async-start(s8[10485760]{0:T(1024)(128)(4,1)} %bitcast.179), calls=%async_computation.11 | async-start | bytes 8388608
  87.2 7.1 %slice-start.2 = ((s8[10485760]{0:T(1024)(128)(4,1)}), s8[4194304]{0:T(1024)(128)(4,1)S(1)}, s32[]{:S(2)}) async-start(s8[10485760]{0:T(1024)(128)(4,1)} %bitcast.179), calls=%async_computation.12 | async-start | bytes 8388608
  129.7 6.5 %slice-start.9 = ((s8[10485760]{0:T(1024)(128)(4,1)}), s8[2097152]{0:T(1024)(128)(4,1)S(1)}, s32[]{:S(2)}) async-start(s8[10485760]{0:T(1024)(128)(4,1)} %bitcast.185), calls=%async_computation.19 | async-start | bytes 4194304
  130.3 6.0 %slice-start.10 = ((s8[10485760]{0:T(1024)(128)(4,1)}), s8[4194304]{0:T(1024)(128)(4,1)S(1)}, s32[]{:S(2)}) async-start(s8[10485760]{0:T(1024)(128)(4,1)} %bitcast.185), calls=%async_computation.20 | async-start | bytes 8388608
  130.3 6.7 %slice-start.11 = ((s8[10485760]{0:T(1024)(128)(4,1)}), s8[4194304]{0:T(1024)(128)(4,1)S(1)}, s32[]{:S(2)}) async-start(s8[10485760]{0:T(1024)(128)(4,1)} %bitcast.185), calls=%async_computation.21 | async-start | bytes 8388608
  135.6 1.4 copy-start.2
  141.5 36.3 %all-to-all-start.5 = ((bf16[4,2,32,1280]{3,2,1,0:T(8,128)(2,1)}), bf16[4,2,32,1280]{3,2,1,0:T(8,128)(2,1)S(1)}, u32[]{:S(2)}, u32[]{:S(2)}) async-start(bf16[4,2,32,1280]{3,2,1,0:T(8,128)(2,1)} %broadcast_in_dim.23), calls=%async_computation.5 | async-start | bytes 1310720 | tf_op jit(solution)/shard_map/all_to_all | solution.py:31
  177.8 17.6 %slice-start.3 = ((s8[10485760]{0:T(1024)(128)(4,1)}), s8[2097152]{0:T(1024)(128)(4,1)S(1)}, s32[]{:S(2)}) async-start(s8[10485760]{0:T(1024)(128)(4,1)} %bitcast.181), calls=%async_computation.13 | async-start | bytes 4194304
  189.4 6.0 %slice-start.4 = ((s8[10485760]{0:T(1024)(128)(4,1)}), s8[4194304]{0:T(1024)(128)(4,1)S(1)}, s32[]{:S(2)}) async-start(s8[10485760]{0:T(1024)(128)(4,1)} %bitcast.181), calls=%async_computation.14 | async-start | bytes 8388608
  189.4 6.5 %slice-start.5 = ((s8[10485760]{0:T(1024)(128)(4,1)}), s8[4194304]{0:T(1024)(128)(4,1)S(1)}, s32[]{:S(2)}) async-start(s8[10485760]{0:T(1024)(128)(4,1)} %bitcast.181), calls=%async_computation.15 | async-start | bytes 8388608
  201.1 15.1 %all-to-all-start.7 = ((bf16[32,2,32,128]{3,2,1,0:T(8,128)(2,1)}), bf16[32,2,32,128]{3,2,1,0:T(8,128)(2,1)S(1)}, u32[]{:S(2)}, u32[]{:S(2)}) async-start(bf16[32,2,32,128]{3,2,1,0:T(8,128)(2,1)} %copy.251), calls=%async_computation.7 | async-start | bytes 1048576 | tf_op jit(solution)/shard_map/all_to_all | solution.py:19
  249.7 4.2 %copy-start.3 = (s32[160]{0:T(256)S(1)}, s32[160]{0:T(256)}, u32[]{:S(2)}) copy-start(s32[160]{0:T(256)} %param.9) | copy-start | bytes 1924
  249.7 38.8 %all-to-all-start.8 = ((f32[32,2,8,1280]{3,2,1,0:T(8,128)}), f32[32,2,8,1280]{3,2,1,0:T(8,128)S(1)}, u32[]{:S(2)}, u32[]{:S(2)}) async-start(f32[32,2,8,1280]{3,2,1,0:T(8,128)} %broadcast_in_dim.25), calls=%async_computation.8 | async-start | bytes 5242880 | tf_op jit(solution)/shard_map/all_to_all | solution.py:31
